TPU v7x, 256 devices: a whole 4x4x8 slice. The times are simulated.
256 devices in a mesh: ens: 16 (over x_lo, z), mesh: 16 (over y, x_hi, core).
Axes of the slice: x: 4 (x_hi: 2, x_lo: 2; x = x_hi * 2 + x_lo), y: 4, z: 8, core: 2. Of those that a mesh axis runs over, the one named last changes fastest.
Arguments:
- inputs: bfloat16 [16, 4096, 512], P('ens', 'mesh'), may hold values from -6 to 6
- cotangent: bfloat16 [16, 4096, 512], P('ens', 'mesh'), may hold values from -6 to 6
- noise_level: float32 [16], P('ens'), may hold values from 0.02 to 80
- neighbours: int32 [4096, 32], P('mesh'), may hold values from 0 to 4095, as said below
- live_slots: int32 [4096, 32], P('mesh'), may hold values from 0 to 1
- projections: bfloat16 [2, 4, 512, 512], replicated, may hold values from -4 to 4
- film_weights: float32 [2, 32, 1024], replicated, may hold values from -0.5 to 0.5
Outputs:
- grad_input: bfloat16 [16, 4096, 512], P('ens', 'mesh')
- grad_projections: float32 [2, 4, 512, 512], P(None, None, 'ens', 'mesh')
- grad_film: float32 [2, 32, 1024], P(None, None, 'mesh')
Inputs may be any that keep to these rules, and one draw needn't show every extreme that they name: `neighbours`: slot 0 of node i names i and is live. The live slots of a node name distinct nodes within 128 of it; every node at least 128 from both ends of the numbering has a live slot exactly 128 away. Padded slots name the node itself.
All inputs are finite; a program needn't handle non-finite values.
Results may differ from a plain program's by a relative error of at most 0.028.
Values may be sent and summed in bfloat16 or wider, within the bound.
A program may use at most 64 MiB of HBM per device.

v0:
```python
import math
import jax
import jax.numpy as jnp
from jax import lax
from jax.sharding import PartitionSpec as P

HEADS = 4
NOISE_FREQ = 16
LAYERS = 2
epsilon = 1e-05


def padded(cells, sides, width):
    for axis, dim in sides:
        count = lax.axis_size(axis)
        ends = count - 1
        head = lax.slice_in_dim(cells, 0, width, axis=dim)
        tail = lax.slice_in_dim(cells, cells.shape[dim] - width, cells.shape[dim], axis=dim)
        cells = jnp.concatenate(
            [
                lax.ppermute(tail, axis, [(i, (i + 1) % count) for i in range(ends)]),
                cells,
                lax.ppermute(head, axis, [((i + 1) % count, i) for i in range(ends)]),
            ],
            axis=dim,
        )
    return cells


def from_behind(block, axis, distance):
    devices = range(lax.axis_size(axis))
    route = [(i - distance, i) for i in devices if i - distance in devices]
    return lax.ppermute(block, axis, route)


def noise_features(noise_level):
    frequency = jnp.arange(1, NOISE_FREQ + 1).astype(jnp.float32)
    angles = jnp.log(noise_level)[:, None] * frequency[None, :]
    return jnp.concatenate([jnp.sin(angles), jnp.cos(angles)], axis=1)


def project(left_side, right_side):
    return jnp.dot(left_side, right_side, preferred_element_type=jnp.float32)


def contract_rows(left_side, right_side):
    return lax.dot_general(
        left_side, right_side, (((0,), (0,)), ((), ())), preferred_element_type=jnp.float32
    )


def contract_cols(left_side, right_side):
    return lax.dot_general(
        left_side, right_side, (((1,), (1,)), ((), ())), preferred_element_type=jnp.float32
    )


def normalize(states, film_row, model_width):
    values = states.astype(jnp.float32)
    centre = jnp.mean(values, axis=1, keepdims=True)
    spread = jnp.mean(jnp.square(values - centre), axis=1, keepdims=True)
    inverse = lax.rsqrt(spread + epsilon)
    unit_rows = (values - centre) * inverse
    normed = (unit_rows * (1.0 + film_row[:model_width]) + film_row[model_width:]).astype(
        jnp.bfloat16
    )
    return (unit_rows, inverse, normed)


def dense_attention(query_head, key_head, present, head_size):
    scores = contract_cols(query_head, key_head) / math.sqrt(head_size)
    scores = jnp.where(present, scores, -jnp.inf)
    row_peak = jnp.max(scores, axis=1, keepdims=True)
    weights = jnp.where(present, jnp.exp(scores - row_peak), 0.0)
    return weights / jnp.sum(weights, axis=1, keepdims=True)


def extend_rims(normed, weights, rim_width, model_width):
    joined = jnp.concatenate(
        [
            project(normed, weights[1]).astype(jnp.bfloat16),
            project(normed, weights[2]).astype(jnp.bfloat16),
        ],
        axis=1,
    )
    joined_ext = padded(joined, (("mesh", 0),), rim_width)
    key_ext = joined_ext[:, :model_width]
    value_ext = joined_ext[:, model_width:]
    return (key_ext, value_ext)


def body(inputs, cotangent, noise_level, neighbours, live_slots, projections, film_weights):
    current = inputs[0]
    node_count, model_width = current.shape
    head_size = model_width // HEADS
    rim_width = node_count // 2
    window = node_count + 2 * rim_width
    offset = lax.axis_index("mesh") * node_count - rim_width
    columns = neighbours - offset
    row_ids = jnp.broadcast_to(jnp.arange(node_count, dtype=jnp.int32)[:, None], columns.shape)
    adjacency = (
        jnp.zeros((node_count, window), jnp.float32)
        .at[row_ids, columns]
        .add(live_slots.astype(jnp.float32))
    )
    present = adjacency > 0.5
    embedding = noise_features(noise_level)[0]
    film_rows = [
        jnp.dot(embedding[None, :], film_weights[layer_number], precision=lax.Precision.HIGHEST)[0]
        for layer_number in range(LAYERS)
    ]
    stored = []
    for layer_number in range(LAYERS):
        weights = projections[layer_number]
        unit_rows, inverse, normed = normalize(current, film_rows[layer_number], model_width)
        queries = project(normed, weights[0]).astype(jnp.bfloat16)
        key_ext, value_ext = extend_rims(normed, weights, rim_width, model_width)
        pieces = []
        for head_index in range(HEADS):
            head_cols = slice(head_index * head_size, (head_index + 1) * head_size)
            attention = dense_attention(
                queries[:, head_cols], key_ext[:, head_cols], present, head_size
            )
            pieces.append(project(attention.astype(jnp.bfloat16), value_ext[:, head_cols]))
        attended = jnp.concatenate(pieces, axis=1).astype(jnp.bfloat16)
        stored.append((unit_rows, inverse, normed, queries, key_ext, value_ext, attended))
        current = (current.astype(jnp.float32) + project(attended, weights[3])).astype(jnp.bfloat16)
    upstream = cotangent[0]
    weight_list = [None] * LAYERS
    film_list = [None] * LAYERS
    for layer_number in reversed(range(LAYERS)):
        weights = projections[layer_number]
        film_row = film_rows[layer_number]
        unit_rows, inverse, normed, queries, key_ext, value_ext, attended = stored[layer_number]
        grad_out = contract_rows(attended, upstream)
        grad_attended = contract_cols(upstream, weights[3]).astype(jnp.bfloat16)
        query_parts, key_parts, value_parts = ([], [], [])
        for head_index in range(HEADS):
            head_cols = slice(head_index * head_size, (head_index + 1) * head_size)
            attention = dense_attention(
                queries[:, head_cols], key_ext[:, head_cols], present, head_size
            )
            rounded = attention.astype(jnp.bfloat16)
            grad_head = grad_attended[:, head_cols]
            grad_probs = contract_cols(grad_head, value_ext[:, head_cols])
            grad_scores = (
                attention
                * (grad_probs - jnp.sum(attention * grad_probs, axis=1, keepdims=True))
                / math.sqrt(head_size)
            ).astype(jnp.bfloat16)
            query_parts.append(project(grad_scores, key_ext[:, head_cols]))
            key_parts.append(contract_rows(grad_scores, queries[:, head_cols]))
            value_parts.append(contract_rows(rounded, grad_head))
        grad_queries = jnp.concatenate(query_parts, axis=1).astype(jnp.bfloat16)
        rim_terms = jnp.concatenate(key_parts + value_parts, axis=1)
        from_above = from_behind(rim_terms[:rim_width].astype(jnp.bfloat16), "mesh", -1).astype(
            jnp.float32
        )
        from_below = from_behind(
            rim_terms[rim_width + node_count :].astype(jnp.bfloat16), "mesh", 1
        ).astype(jnp.float32)
        owned_rows = rim_terms[rim_width : rim_width + node_count]
        owned_rows = (
            owned_rows
            + jnp.pad(from_below, ((0, node_count - rim_width), (0, 0)))
            + jnp.pad(from_above, ((node_count - rim_width, 0), (0, 0)))
        )
        grad_keys = owned_rows[:, :model_width].astype(jnp.bfloat16)
        grad_values = owned_rows[:, model_width:].astype(jnp.bfloat16)
        weight_list[layer_number] = jnp.stack(
            [
                contract_rows(normed, grad_queries),
                contract_rows(normed, grad_keys),
                contract_rows(normed, grad_values),
                grad_out,
            ]
        )
        grad_normed = (
            contract_cols(grad_queries, weights[0])
            + contract_cols(grad_keys, weights[1])
            + contract_cols(grad_values, weights[2])
        )
        grad_conditioning = jnp.concatenate(
            [jnp.sum(grad_normed * unit_rows, axis=0), jnp.sum(grad_normed, axis=0)]
        )
        film_list[layer_number] = embedding[:, None] * grad_conditioning[None, :]
        grad_unit = grad_normed * (1.0 + film_row[:model_width])
        centred = (
            grad_unit
            - jnp.mean(grad_unit, axis=1, keepdims=True)
            - unit_rows * jnp.mean(grad_unit * unit_rows, axis=1, keepdims=True)
        )
        upstream = (upstream.astype(jnp.float32) + inverse * centred).astype(jnp.bfloat16)
    weight_grads = jnp.stack(weight_list)
    film_grads = jnp.stack(film_list)
    weight_part, film_part = (
        lax.psum_scatter(
            weight_grads.astype(jnp.bfloat16), "mesh", scatter_dimension=3, tiled=True
        ).astype(jnp.float32),
        lax.psum_scatter(
            film_grads.astype(jnp.bfloat16), "mesh", scatter_dimension=2, tiled=True
        ).astype(jnp.float32),
    )
    weight_out = lax.psum_scatter(
        weight_part.astype(jnp.bfloat16), "ens", scatter_dimension=2, tiled=True
    ).astype(jnp.float32)
    film_out = lax.psum(film_part, "ens")
    return (upstream[None], weight_out, film_out)


def solution(mesh):
    placed = (
        P("ens", "mesh", None),
        P("ens", "mesh", None),
        P("ens"),
        P("mesh", None),
        P("mesh", None),
        P(),
        P(),
    )
    return jax.shard_map(
        body,
        mesh=mesh,
        in_specs=placed,
        out_specs=(P("ens", "mesh", None), P(None, None, "ens", "mesh"), P(None, None, "mesh")),
        check_vma=False,
    )
```

profile of v0, /device:TPU:8, one launch (start us, length us, event | category | flops | bytes accessed | tf_op | source)
XLA Modules:
  0.0 475.2 jit_solution(4812661853184379244)
XLA Ops:
  8.0 1.1 convert_reduce_fusion
  9.1 1.2 fusion.37
  10.2 1.1 fusion.115
  11.5 1.6 convolution_convert_fusion.14
  13.0 1.4 convolution_convert_fusion.13
  14.5 1.9 collective-permute-start
  16.4 6.0 %collective-permute-start.1 = (bf16[128,1024]{1,0:T(8,128)(2,1)S(1)}, bf16[128,1024]{1,0:T(8,128)(2,1)S(1)}, u32[]{:S(2)}, u32[]{:S(2)}) collective-permute-start(bf16[128,1024]{1,0:T(8,128)(2,1)S(1)} %get-tuple-element.40), channel_id=1, source_target_pairs={{1,0},{2,1},{3,2},{4,3},{5,4},{6,5},{7,6},{8,7},{9,8},{10,9},{11,1... | collective-permute-start | bytes 786440 | tf_op jit(solution)/shard_map/ppermute | solution.py:23
  23.4 56.7 %scatter_custom_fusion = f32[131072]{0:T(1024)S(1)} fusion(s32[8192]{0:T(1024)S(1)} %reshape.328, f32[8192]{0:T(1024)S(1)} %reshape.330, f32[]{:T(128)} %constant.46.clone.1), kind=kCustom, calls=%fused_computation.217 | custom fusion | flops 8192 | bytes 524292
  80.4 1.4 convolution_convert_fusion.15
  83.2 0.7 fusion.75
  84.0 0.5 fusion.74
  85.4 0.7 copy-done.1
  87.7 1.9 collective-permute-start.2
  89.6 6.2 %collective-permute-start.3 = (bf16[128,1024]{1,0:T(8,128)(2,1)S(1)}, bf16[128,1024]{1,0:T(8,128)(2,1)S(1)}, u32[]{:S(2)}, u32[]{:S(2)}) collective-permute-start(bf16[128,1024]{1,0:T(8,128)(2,1)S(1)} %get-tuple-element.38), channel_id=1, source_target_pairs={{1,0},{2,1},{3,2},{4,3},{5,4},{6,5},{7,6},{8,7},{9,8},{10,9},{11,1... | collective-permute-start | bytes 786440 | tf_op jit(solution)/shard_map/ppermute | solution.py:23
  96.5 1.3 collective-permute-done.2
  97.7 1.8 collective-permute-done.3
  101.7 0.7 fusion.83
  102.4 0.9 multiply_reduce_fusion.9
  107.8 3.4 collective-permute-start.4
  111.2 4.7 collective-permute-start.5
  117.0 1.2 collective-permute-done.4
  118.2 1.6 collective-permute-done.5
  120.3 0.6 multiply_reduce_fusion
  127.1 2.9 collective-permute-start.6
  130.0 5.5 %collective-permute-start.7 = (bf16[128,1024]{0,1:T(8,128)(2,1)S(1)}, bf16[128,1024]{0,1:T(8,128)(2,1)S(1)}, u32[]{:S(2)}, u32[]{:S(2)}) collective-permute-start(bf16[128,1024]{0,1:T(8,128)(2,1)S(1)} %get-tuple-element.34), channel_id=1, source_target_pairs={{1,0},{2,1},{3,2},{4,3},{5,4},{6,5},{7,6},{8,7},{9,8},{10,9},{11,1... | collective-permute-start | bytes 786440 | tf_op jit(solution)/shard_map/ppermute | solution.py:33
  135.4 0.5 fusion
  136.6 0.9 collective-permute-done.6
  137.5 1.6 collective-permute-done.7
  139.8 0.5 fusion.2
  140.5 2.3 pad_maximum_fusion
  142.9 7.9 %copy.17 = bf16[2,4,512,512]{2,1,0,3:T(4,128)(2,1)} copy(bf16[2,4,512,512]{3,2,1,0:T(8,128)(2,1)} %pad_maximum_fusion) | data formatting | bytes 8388608 | tf_op jit(solution)/shard_map/stack | solution.py:194
  150.9 1.4 fusion.56
  152.3 1.4 convolution_add_fusion.1
  153.7 1.6 fusion.36
  155.9 1.0 reshape.340
  156.9 0.6 dynamic-slice
  158.2 152.6 %all-reduce.7.cloned.1.call-done = bf16[2,4,512,512]{2,1,0,3:T(4,128)(2,1)} async-done(((bf16[2,4,512,512]{2,1,0,3:T(4,128)(2,1)}), bf16[2,4,512,512]{2,1,0,3:T(4,128)(2,1)}) %all-reduce.7.cloned.1.call-update) | async-done | bytes 4194320
  310.7 1.0 constant_dynamic-slice_fusion
  311.8 14.2 %copy.19 = bf16[2,4,512,32]{1,0,3,2:T(2,128)(2,1)} copy(bf16[2,4,512,32]{2,1,0,3:T(4,128)(2,1)S(1)} %constant_dynamic-slice_fusion) | data formatting | bytes 524288
  325.9 17.2 %reshape.338 = bf16[512,256]{1,0:T(8,128)(2,1)} reshape(bf16[512,32,2,4]{3,2,1,0:T(2,128)(2,1)} %bitcast.167) | data formatting | bytes 524288
  343.2 1.0 fusion.93
  344.2 49.2 %reduce-scatter.9.cloned.1.call-done = bf16[64,64]{1,0:T(8,128)(2,1)} async-done(((bf16[1024,64]{1,0:T(8,128)(2,1)}), bf16[64,64]{1,0:T(8,128)(2,1)}) %reduce-scatter.9.cloned.1.call-update) | async-done | bytes 8208
  393.3 0.8 reshape.341
  394.2 63.6 %psum.7 = f32[2,32,64]{2,1,0:T(8,128)} all-reduce(bf16[2,32,64]{2,1,0:T(8,128)(2,1)S(1)} %copy.22), channel_id=1, replica_groups=mesh['ens'=16,'mesh'=16] {'ens'}, use_global_device_ids=true, to_apply=%region_40.41 | all-reduce | flops 4096 | bytes 24576 | tf_op jit(solution)/shard_map/psum | solution.py:207
  457.9 7.4 %reduce-scatter.7.cloned.1.call-done = bf16[32,256]{1,0:T(8,128)(2,1)} async-done(((bf16[512,256]{1,0:T(8,128)(2,1)}), bf16[32,256]{1,0:T(8,128)(2,1)}) %reduce-scatter.7.cloned.1.call-update) | async-done | bytes 16400
  465.2 1.8 reshape.339
  467.1 0.8 copy.20
  467.9 0.8 copy.18
  (140 shorter events, 22.0 us)
Async XLA Ops:
  7.2 5.9 %copy-start = (bf16[1,256,512]{2,1,0:T(8,128)(2,1)S(1)}, bf16[1,256,512]{2,1,0:T(8,128)(2,1)}, u32[]{:S(2)}) copy-start(bf16[1,256,512]{2,1,0:T(8,128)(2,1)} %param.7) | copy-start | bytes 786436
  7.2 303.5 %all-reduce.7.cloned.1.call-start = ((), (), s32[]{:S(2)}) async-start(), calls=%async_computation.4 | async-start | bytes 8388608
  11.4 11.1 %copy-start.2 = (f32[2,32,1024]{2,1,0:T(8,128)S(1)}, f32[2,32,1024]{2,1,0:T(8,128)}, u32[]{:S(2)}) copy-start(f32[2,32,1024]{2,1,0:T(8,128)} %param.13) | copy-start | bytes 786436
  11.4 11.3 %copy-start.4 = (s32[256,32]{0,1:T(8,128)S(1)}, s32[256,32]{0,1:T(8,128)}, u32[]{:S(2)}) copy-start(s32[256,32]{0,1:T(8,128)} %param.10) | copy-start | bytes 98308
  11.4 11.4 %copy-start.7 = (s32[2]{0:T(128)S(1)}, s32[2]{0:T(128)}, u32[]{:S(2)}) copy-start(s32[2]{0:T(128)} %constant.74) | copy-start | bytes 28
  11.4 11.4 %copy-start.6 = (s32[2]{0:T(128)S(1)}, s32[2]{0:T(128)}, u32[]{:S(2)}) copy-start(s32[2]{0:T(128)} %constant.71) | copy-start | bytes 28
  11.5 11.5 %copy-start.5 = (s32[256,32]{0,1:T(8,128)S(1)}, s32[256,32]{0,1:T(8,128)}, u32[]{:S(2)}) copy-start(s32[256,32]{0,1:T(8,128)} %param.11) | copy-start | bytes 98308
  14.5 67.3 %collective-permute-start = (bf16[128,1024]{1,0:T(8,128)(2,1)S(1)}, bf16[128,1024]{1,0:T(8,128)(2,1)S(1)}, u32[]{:S(2)}, u32[]{:S(2)}) collective-permute-start(bf16[128,1024]{1,0:T(8,128)(2,1)S(1)} %get-tuple-element.39), channel_id=1, source_target_pairs={{0,1},{1,2},{2,3},{3,4},{4,5},{5,6},{6,7},{7,8},{8,9},{9,10},{10,1... | collective-permute-start | bytes 786440 | tf_op jit(solution)/shard_map/ppermute | solution.py:21
  16.4 65.4 %collective-permute-start.1 = (bf16[128,1024]{1,0:T(8,128)(2,1)S(1)}, bf16[128,1024]{1,0:T(8,128)(2,1)S(1)}, u32[]{:S(2)}, u32[]{:S(2)}) collective-permute-start(bf16[128,1024]{1,0:T(8,128)(2,1)S(1)} %get-tuple-element.40), channel_id=1, source_target_pairs={{1,0},{2,1},{3,2},{4,3},{5,4},{6,5},{7,6},{8,7},{9,8},{10,9},{11,1... | collective-permute-start | bytes 786440 | tf_op jit(solution)/shard_map/ppermute | solution.py:23
  84.0 2.2 copy-start.1
  86.8 9.0 %copy-start.3 = (bf16[1,256,512]{2,1,0:T(8,128)(2,1)S(1)}, bf16[1,256,512]{2,1,0:T(8,128)(2,1)}, u32[]{:S(2)}) copy-start(bf16[1,256,512]{2,1,0:T(8,128)(2,1)} %param.8) | copy-start | bytes 786436
  87.7 10.1 %collective-permute-start.2 = (bf16[128,1024]{1,0:T(8,128)(2,1)S(1)}, bf16[128,1024]{1,0:T(8,128)(2,1)S(1)}, u32[]{:S(2)}, u32[]{:S(2)}) collective-permute-start(bf16[128,1024]{1,0:T(8,128)(2,1)S(1)} %get-tuple-element.37), channel_id=1, source_target_pairs={{0,1},{1,2},{2,3},{3,4},{4,5},{5,6},{6,7},{7,8},{8,9},{9,10},{10,1... | collective-permute-start | bytes 786440 | tf_op jit(solution)/shard_map/ppermute | solution.py:21
  89.6 9.9 %collective-permute-start.3 = (bf16[128,1024]{1,0:T(8,128)(2,1)S(1)}, bf16[128,1024]{1,0:T(8,128)(2,1)S(1)}, u32[]{:S(2)}, u32[]{:S(2)}) collective-permute-start(bf16[128,1024]{1,0:T(8,128)(2,1)S(1)} %get-tuple-element.38), channel_id=1, source_target_pairs={{1,0},{2,1},{3,2},{4,3},{5,4},{6,5},{7,6},{8,7},{9,8},{10,9},{11,1... | collective-permute-start | bytes 786440 | tf_op jit(solution)/shard_map/ppermute | solution.py:23
  107.8 10.4 %collective-permute-start.4 = (bf16[128,1024]{0,1:T(8,128)(2,1)S(1)}, bf16[128,1024]{0,1:T(8,128)(2,1)S(1)}, u32[]{:S(2)}, u32[]{:S(2)}) collective-permute-start(bf16[128,1024]{0,1:T(8,128)(2,1)S(1)} %get-tuple-element.35), channel_id=1, source_target_pairs={{0,1},{1,2},{2,3},{3,4},{4,5},{5,6},{6,7},{7,8},{8,9},{9,10},{10,1... | collective-permute-start | bytes 786440 | tf_op jit(solution)/shard_map/ppermute | solution.py:33
  111.2 8.6 %collective-permute-start.5 = (bf16[128,1024]{0,1:T(8,128)(2,1)S(1)}, bf16[128,1024]{0,1:T(8,128)(2,1)S(1)}, u32[]{:S(2)}, u32[]{:S(2)}) collective-permute-start(bf16[128,1024]{0,1:T(8,128)(2,1)S(1)} %get-tuple-element.36), channel_id=1, source_target_pairs={{1,0},{2,1},{3,2},{4,3},{5,4},{6,5},{7,6},{8,7},{9,8},{10,9},{11,1... | collective-permute-start | bytes 786440 | tf_op jit(solution)/shard_map/ppermute | solution.py:33
  127.1 10.4 %collective-permute-start.6 = (bf16[128,1024]{0,1:T(8,128)(2,1)S(1)}, bf16[128,1024]{0,1:T(8,128)(2,1)S(1)}, u32[]{:S(2)}, u32[]{:S(2)}) collective-permute-start(bf16[128,1024]{0,1:T(8,128)(2,1)S(1)} %get-tuple-element.33), channel_id=1, source_target_pairs={{0,1},{1,2},{2,3},{3,4},{4,5},{5,6},{6,7},{7,8},{8,9},{9,10},{10,1... | collective-permute-start | bytes 786440 | tf_op jit(solution)/shard_map/ppermute | solution.py:33
  130.0 9.1 %collective-permute-start.7 = (bf16[128,1024]{0,1:T(8,128)(2,1)S(1)}, bf16[128,1024]{0,1:T(8,128)(2,1)S(1)}, u32[]{:S(2)}, u32[]{:S(2)}) collective-permute-start(bf16[128,1024]{0,1:T(8,128)(2,1)S(1)} %get-tuple-element.34), channel_id=1, source_target_pairs={{1,0},{2,1},{3,2},{4,3},{5,4},{6,5},{7,6},{8,7},{9,8},{10,9},{11,1... | collective-permute-start | bytes 786440 | tf_op jit(solution)/shard_map/ppermute | solution.py:33
  150.8 242.5 %reduce-scatter.9.cloned.1.call-start = ((), (), s32[]{:S(2)}) async-start(), calls=%async_computation.3 | async-start | bytes 278528
  153.7 3.2 copy-start.8
  156.9 308.4 %reduce-scatter.7.cloned.1.call-start = ((), (), s32[]{:S(2)}) async-start(), calls=%async_computation.2 | async-start | bytes 278528
Sparse Core Ops, SparseCore 0:
  150.9 159.7 all-reduce.6
  314.7 78.6 reduce-scatter.8
  395.8 69.3 reduce-scatter.6
where the time goes:
time: 476 us; the launch traced here: 475 us
  waiting for transfers between devices  218 us (46%)
  other arithmetic  67.9 us (14%)
  blocking collectives  63.6 us (13%)
  local copies, waits for them, and re-layouts  47.9 us (10%)
  starting transfers between devices  32.7 us (7%)
  matrix products  29.3 us (6%)
  between operations  16.1 us (3%)
    unnamed x6, waiting for transfers between devices  209 us
    psum x1, blocking collectives, body(): film_out = lax.psum(film_part, 'ens')  63.6 us
    unnamed x4, other arithmetic  56.9 us
    unnamed x31, local copies, waits for them, and re-layouts  39.6 us
    ppermute x4, starting transfers between devices, from_behind(): return lax.ppermute(block, axis, route)  16.5 us
    ppermute x2, starting transfers between devices, padded(): lax.ppermute(head, axis, [((i + 1) % count, i) for i in range(ends)])  12.3 us
    dot_general x24, matrix products, contract_cols(): lax.dot_general(left_side, right_side, (((1,), (1,)), ((), ())), preferre...  11.8 us
  transfers between devices with their start and end apart: 11, of which 9 were waited for; matrix products, arithmetic and copies ran while one was open for 22% of the time, Pallas kernels for 0%

commit v1 on v0

--- a/solution.py
+++ b/solution.py
@@ -204,7 +204,7 @@
     weight_out = lax.psum_scatter(
         weight_part.astype(jnp.bfloat16), "ens", scatter_dimension=2, tiled=True
     ).astype(jnp.float32)
-    film_out = lax.psum(film_part, "ens")
+    film_out = jnp.sum(lax.all_gather(film_part, "ens"), axis=0)
     return (upstream[None], weight_out, film_out)
 
 

time: 476 us -> 476 us (level)
  blocking collectives: 63.6 us -> 36.1 us
  waiting for transfers between devices: 218 us -> 244 us
    psum x1 -> x0, blocking collectives: 63.6 us -> none  [body(): film_out = lax.psum(film_part, 'ens')]
    all_gather x0 -> x1, blocking collectives: none -> 36.1 us  [body(): film_out = jnp.sum(lax.all_gather(film_part, 'ens'), axis=0)]
    unnamed x6, waiting for transfers between devices: 209 us -> 235 us
where the time goes in v1:
time: 476 us; the launch traced here: 475 us
  waiting for transfers between devices  244 us (51%)
  other arithmetic  68.6 us (14%)
  local copies, waits for them, and re-layouts  48.5 us (10%)
  blocking collectives  36.1 us (8%)
  starting transfers between devices  32.7 us (7%)
  matrix products  29.3 us (6%)
  between operations  16.1 us (3%)
    unnamed x6, waiting for transfers between devices  235 us
    unnamed x4, other arithmetic  56.9 us
    unnamed x31, local copies, waits for them, and re-layouts  40.2 us
    all_gather x1, blocking collectives, body(): film_out = jnp.sum(lax.all_gather(film_part, 'ens'), axis=0)  36.1 us
    ppermute x4, starting transfers between devices, from_behind(): return lax.ppermute(block, axis, route)  16.5 us
    ppermute x2, starting transfers between devices, padded(): lax.ppermute(head, axis, [((i + 1) % count, i) for i in range(ends)])  12.3 us
    dot_general x24, matrix products, contract_cols(): lax.dot_general(left_side, right_side, (((1,), (1,)), ((), ())), preferre...  11.8 us
  transfers between devices with their start and end apart: 11, of which 9 were waited for; matrix products, arithmetic and copies ran while one was open for 22% of the time, Pallas kernels for 0%

profile of v1, /device:TPU:8, one launch (start us, length us, event | category | flops | bytes accessed | tf_op | source)
XLA Modules:
  0.0 475.1 jit_solution(434420212116050010)
XLA Ops:
  8.0 1.1 convert_reduce_fusion
  9.1 1.2 fusion.37
  10.2 1.1 fusion.115
  11.5 1.6 convolution_convert_fusion.14
  13.0 1.4 convolution_convert_fusion.13
  14.5 1.9 collective-permute-start
  16.4 6.0 %collective-permute-start.1 = (bf16[128,1024]{1,0:T(8,128)(2,1)S(1)}, bf16[128,1024]{1,0:T(8,128)(2,1)S(1)}, u32[]{:S(2)}, u32[]{:S(2)}) collective-permute-start(bf16[128,1024]{1,0:T(8,128)(2,1)S(1)} %get-tuple-element.40), channel_id=1, source_target_pairs={{1,0},{2,1},{3,2},{4,3},{5,4},{6,5},{7,6},{8,7},{9,8},{10,9},{11,1... | collective-permute-start | bytes 786440 | tf_op jit(solution)/shard_map/ppermute | solution.py:23
  23.4 56.7 %scatter_custom_fusion = f32[131072]{0:T(1024)S(1)} fusion(s32[8192]{0:T(1024)S(1)} %reshape.329, f32[8192]{0:T(1024)S(1)} %reshape.331, f32[]{:T(128)} %constant.46.clone.1), kind=kCustom, calls=%fused_computation.217 | custom fusion | flops 8192 | bytes 524292
  80.4 1.4 convolution_convert_fusion.15
  83.2 0.7 fusion.75
  84.0 0.5 fusion.74
  85.4 0.7 copy-done.1
  87.7 1.9 collective-permute-start.2
  89.6 6.2 %collective-permute-start.3 = (bf16[128,1024]{1,0:T(8,128)(2,1)S(1)}, bf16[128,1024]{1,0:T(8,128)(2,1)S(1)}, u32[]{:S(2)}, u32[]{:S(2)}) collective-permute-start(bf16[128,1024]{1,0:T(8,128)(2,1)S(1)} %get-tuple-element.38), channel_id=1, source_target_pairs={{1,0},{2,1},{3,2},{4,3},{5,4},{6,5},{7,6},{8,7},{9,8},{10,9},{11,1... | collective-permute-start | bytes 786440 | tf_op jit(solution)/shard_map/ppermute | solution.py:23
  96.5 1.3 collective-permute-done.2
  97.7 1.8 collective-permute-done.3
  101.7 0.7 fusion.83
  102.4 0.9 multiply_reduce_fusion.9
  107.8 3.4 collective-permute-start.4
  111.2 4.7 collective-permute-start.5
  117.0 1.2 collective-permute-done.4
  118.2 1.6 collective-permute-done.5
  120.3 0.6 multiply_reduce_fusion
  127.1 2.9 collective-permute-start.6
  130.0 5.5 %collective-permute-start.7 = (bf16[128,1024]{0,1:T(8,128)(2,1)S(1)}, bf16[128,1024]{0,1:T(8,128)(2,1)S(1)}, u32[]{:S(2)}, u32[]{:S(2)}) collective-permute-start(bf16[128,1024]{0,1:T(8,128)(2,1)S(1)} %get-tuple-element.34), channel_id=1, source_target_pairs={{1,0},{2,1},{3,2},{4,3},{5,4},{6,5},{7,6},{8,7},{9,8},{10,9},{11,1... | collective-permute-start | bytes 786440 | tf_op jit(solution)/shard_map/ppermute | solution.py:33
  136.6 0.9 collective-permute-done.6
  137.5 1.6 collective-permute-done.7
  140.5 2.3 pad_maximum_fusion
  142.9 7.9 %copy.17 = bf16[2,4,512,512]{2,1,0,3:T(4,128)(2,1)} copy(bf16[2,4,512,512]{3,2,1,0:T(8,128)(2,1)} %pad_maximum_fusion) | data formatting | bytes 8388608 | tf_op jit(solution)/shard_map/stack | solution.py:194
  150.9 0.6 copy-done.8
  151.5 0.6 dynamic-slice
  152.8 1.4 fusion.56
  154.2 1.4 convolution_add_fusion.1
  155.6 1.6 fusion.36
  157.7 1.0 reshape.342
  158.7 152.0 %all-reduce.7.cloned.1.call-done = bf16[2,4,512,512]{2,1,0,3:T(4,128)(2,1)} async-done(((bf16[2,4,512,512]{2,1,0,3:T(4,128)(2,1)}), bf16[2,4,512,512]{2,1,0,3:T(4,128)(2,1)}) %all-reduce.7.cloned.1.call-update) | async-done | bytes 4194320
  310.7 1.0 constant_dynamic-slice_fusion
  311.8 14.2 %copy.19 = bf16[2,4,512,32]{1,0,3,2:T(2,128)(2,1)} copy(bf16[2,4,512,32]{2,1,0,3:T(4,128)(2,1)S(1)} %constant_dynamic-slice_fusion) | data formatting | bytes 524288
  325.9 17.2 %reshape.340 = bf16[512,256]{1,0:T(8,128)(2,1)} reshape(bf16[512,32,2,4]{3,2,1,0:T(2,128)(2,1)} %bitcast.168) | data formatting | bytes 524288
  343.2 1.0 fusion.93
  344.1 49.2 %reduce-scatter.9.cloned.1.call-done = bf16[64,64]{1,0:T(8,128)(2,1)} async-done(((bf16[1024,64]{1,0:T(8,128)(2,1)}), bf16[64,64]{1,0:T(8,128)(2,1)}) %reduce-scatter.9.cloned.1.call-update) | async-done | bytes 8208
  393.3 0.8 reshape.343
  394.2 36.1 %all-gather = f32[32,32,64]{2,1,0:T(8,128)S(1)} all-gather(f32[2,32,64]{2,1,0:T(8,128)S(1)} %all_gather.12), channel_id=2, replica_groups=mesh['ens'=16,'mesh'=16] {'ens'}, dimensions={0}, use_global_device_ids=true | all-gather | bytes 278528 | tf_op jit(solution)/shard_map/all_gather | solution.py:207
  430.4 0.7 reduce_sum.321
  431.0 34.2 %reduce-scatter.7.cloned.1.call-done = bf16[32,256]{1,0:T(8,128)(2,1)} async-done(((bf16[512,256]{1,0:T(8,128)(2,1)}), bf16[32,256]{1,0:T(8,128)(2,1)}) %reduce-scatter.7.cloned.1.call-update) | async-done | bytes 16400
  465.2 1.8 reshape.341
  467.1 0.8 copy.20
  467.9 0.8 copy.18
  (142 shorter events, 23.0 us)
Async XLA Ops:
  7.2 5.9 %copy-start = (bf16[1,256,512]{2,1,0:T(8,128)(2,1)S(1)}, bf16[1,256,512]{2,1,0:T(8,128)(2,1)}, u32[]{:S(2)}) copy-start(bf16[1,256,512]{2,1,0:T(8,128)(2,1)} %param.7) | copy-start | bytes 786436
  7.2 303.5 %all-reduce.7.cloned.1.call-start = ((), (), s32[]{:S(2)}) async-start(), calls=%async_computation.4 | async-start | bytes 8388608
  11.4 11.1 %copy-start.2 = (f32[2,32,1024]{2,1,0:T(8,128)S(1)}, f32[2,32,1024]{2,1,0:T(8,128)}, u32[]{:S(2)}) copy-start(f32[2,32,1024]{2,1,0:T(8,128)} %param.13) | copy-start | bytes 786436
  11.4 11.3 %copy-start.4 = (s32[256,32]{0,1:T(8,128)S(1)}, s32[256,32]{0,1:T(8,128)}, u32[]{:S(2)}) copy-start(s32[256,32]{0,1:T(8,128)} %param.10) | copy-start | bytes 98308
  11.4 11.4 %copy-start.7 = (s32[2]{0:T(128)S(1)}, s32[2]{0:T(128)}, u32[]{:S(2)}) copy-start(s32[2]{0:T(128)} %constant.74) | copy-start | bytes 28
  11.4 11.4 %copy-start.6 = (s32[2]{0:T(128)S(1)}, s32[2]{0:T(128)}, u32[]{:S(2)}) copy-start(s32[2]{0:T(128)} %constant.71) | copy-start | bytes 28
  11.5 11.5 %copy-start.5 = (s32[256,32]{0,1:T(8,128)S(1)}, s32[256,32]{0,1:T(8,128)}, u32[]{:S(2)}) copy-start(s32[256,32]{0,1:T(8,128)} %param.11) | copy-start | bytes 98308
  14.5 67.3 %collective-permute-start = (bf16[128,1024]{1,0:T(8,128)(2,1)S(1)}, bf16[128,1024]{1,0:T(8,128)(2,1)S(1)}, u32[]{:S(2)}, u32[]{:S(2)}) collective-permute-start(bf16[128,1024]{1,0:T(8,128)(2,1)S(1)} %get-tuple-element.39), channel_id=1, source_target_pairs={{0,1},{1,2},{2,3},{3,4},{4,5},{5,6},{6,7},{7,8},{8,9},{9,10},{10,1... | collective-permute-start | bytes 786440 | tf_op jit(solution)/shard_map/ppermute | solution.py:21
  16.4 65.4 %collective-permute-start.1 = (bf16[128,1024]{1,0:T(8,128)(2,1)S(1)}, bf16[128,1024]{1,0:T(8,128)(2,1)S(1)}, u32[]{:S(2)}, u32[]{:S(2)}) collective-permute-start(bf16[128,1024]{1,0:T(8,128)(2,1)S(1)} %get-tuple-element.40), channel_id=1, source_target_pairs={{1,0},{2,1},{3,2},{4,3},{5,4},{6,5},{7,6},{8,7},{9,8},{10,9},{11,1... | collective-permute-start | bytes 786440 | tf_op jit(solution)/shard_map/ppermute | solution.py:23
  84.0 2.2 copy-start.1
  86.8 9.0 %copy-start.3 = (bf16[1,256,512]{2,1,0:T(8,128)(2,1)S(1)}, bf16[1,256,512]{2,1,0:T(8,128)(2,1)}, u32[]{:S(2)}) copy-start(bf16[1,256,512]{2,1,0:T(8,128)(2,1)} %param.8) | copy-start | bytes 786436
  87.7 10.1 %collective-permute-start.2 = (bf16[128,1024]{1,0:T(8,128)(2,1)S(1)}, bf16[128,1024]{1,0:T(8,128)(2,1)S(1)}, u32[]{:S(2)}, u32[]{:S(2)}) collective-permute-start(bf16[128,1024]{1,0:T(8,128)(2,1)S(1)} %get-tuple-element.37), channel_id=1, source_target_pairs={{0,1},{1,2},{2,3},{3,4},{4,5},{5,6},{6,7},{7,8},{8,9},{9,10},{10,1... | collective-permute-start | bytes 786440 | tf_op jit(solution)/shard_map/ppermute | solution.py:21
  89.6 9.9 %collective-permute-start.3 = (bf16[128,1024]{1,0:T(8,128)(2,1)S(1)}, bf16[128,1024]{1,0:T(8,128)(2,1)S(1)}, u32[]{:S(2)}, u32[]{:S(2)}) collective-permute-start(bf16[128,1024]{1,0:T(8,128)(2,1)S(1)} %get-tuple-element.38), channel_id=1, source_target_pairs={{1,0},{2,1},{3,2},{4,3},{5,4},{6,5},{7,6},{8,7},{9,8},{10,9},{11,1... | collective-permute-start | bytes 786440 | tf_op jit(solution)/shard_map/ppermute | solution.py:23
  107.8 10.4 %collective-permute-start.4 = (bf16[128,1024]{0,1:T(8,128)(2,1)S(1)}, bf16[128,1024]{0,1:T(8,128)(2,1)S(1)}, u32[]{:S(2)}, u32[]{:S(2)}) collective-permute-start(bf16[128,1024]{0,1:T(8,128)(2,1)S(1)} %get-tuple-element.35), channel_id=1, source_target_pairs={{0,1},{1,2},{2,3},{3,4},{4,5},{5,6},{6,7},{7,8},{8,9},{9,10},{10,1... | collective-permute-start | bytes 786440 | tf_op jit(solution)/shard_map/ppermute | solution.py:33
  111.2 8.6 %collective-permute-start.5 = (bf16[128,1024]{0,1:T(8,128)(2,1)S(1)}, bf16[128,1024]{0,1:T(8,128)(2,1)S(1)}, u32[]{:S(2)}, u32[]{:S(2)}) collective-permute-start(bf16[128,1024]{0,1:T(8,128)(2,1)S(1)} %get-tuple-element.36), channel_id=1, source_target_pairs={{1,0},{2,1},{3,2},{4,3},{5,4},{6,5},{7,6},{8,7},{9,8},{10,9},{11,1... | collective-permute-start | bytes 786440 | tf_op jit(solution)/shard_map/ppermute | solution.py:33
  127.1 10.4 %collective-permute-start.6 = (bf16[128,1024]{0,1:T(8,128)(2,1)S(1)}, bf16[128,1024]{0,1:T(8,128)(2,1)S(1)}, u32[]{:S(2)}, u32[]{:S(2)}) collective-permute-start(bf16[128,1024]{0,1:T(8,128)(2,1)S(1)} %get-tuple-element.33), channel_id=1, source_target_pairs={{0,1},{1,2},{2,3},{3,4},{4,5},{5,6},{6,7},{7,8},{8,9},{9,10},{10,1... | collective-permute-start | bytes 786440 | tf_op jit(solution)/shard_map/ppermute | solution.py:33
  130.0 9.1 %collective-permute-start.7 = (bf16[128,1024]{0,1:T(8,128)(2,1)S(1)}, bf16[128,1024]{0,1:T(8,128)(2,1)S(1)}, u32[]{:S(2)}, u32[]{:S(2)}) collective-permute-start(bf16[128,1024]{0,1:T(8,128)(2,1)S(1)} %get-tuple-element.34), channel_id=1, source_target_pairs={{1,0},{2,1},{3,2},{4,3},{5,4},{6,5},{7,6},{8,7},{9,8},{10,9},{11,1... | collective-permute-start | bytes 786440 | tf_op jit(solution)/shard_map/ppermute | solution.py:33
  150.8 0.7 copy-start.8
  150.8 242.5 %reduce-scatter.9.cloned.1.call-start = ((), (), s32[]{:S(2)}) async-start(), calls=%async_computation.3 | async-start | bytes 278528
  158.7 306.5 %reduce-scatter.7.cloned.1.call-start = ((), (), s32[]{:S(2)}) async-start(), calls=%async_computation.2 | async-start | bytes 278528
Sparse Core Ops, SparseCore 0:
  150.9 159.7 all-reduce.6
  314.7 78.6 reduce-scatter.8
  395.8 69.3 reduce-scatter.6
